TPU v7x, 256 devices: a whole 4x4x8 slice. The times are simulated.
256 devices in a mesh: row: 16 (over y_hi, x, core), rep: 16 (over y_lo, z).
Axes of the slice: x: 4, y: 4 (y_hi: 2, y_lo: 2; y = y_hi * 2 + y_lo), z: 8, core: 2. Of those that a mesh axis runs over, the one named last changes fastest.
Arguments:
- features: bfloat16 [65536, 512], P(('row', 'rep')), may hold values from -6 to 6
- tiles: bfloat16 [512, 8, 128, 128], P(('row', 'rep')), may hold values from -0.1875 to 0.1875
- columns: int32 [512, 8], P(('row', 'rep')), may hold values from 0 to 511, as said below
- w_aggregate: bfloat16 [512, 512], replicated, may hold values from -0.25 to 0.25
- w_self: bfloat16 [512, 512], replicated, may hold values from -0.25 to 0.25
- w_middle: bfloat16 [512, 512], replicated, may hold values from -0.25 to 0.25
- w_output: bfloat16 [512, 512], replicated, may hold values from -0.25 to 0.25
- cotangent: bfloat16 [65536, 512], P(('row', 'rep')), may hold values from -6 to 6
Outputs:
- updated: bfloat16 [65536, 512], P(('row', 'rep'))
- grad_features: bfloat16 [65536, 512], P(('row', 'rep'))
- grad_output: float32 [512, 512], P('rep')
- grad_middle: float32 [512, 512], P('rep')
- grad_aggregate: float32 [512, 512], P('rep')
- grad_self: float32 [512, 512], P('rep')
Inputs may be any that keep to these rules, and one draw needn't show every extreme that they name: `columns`: row group g holds row blocks g * 32 to (g + 1) * 32 - 1, for g < 16. Every column block named by a row block of group g lies in group g - 1, g or g + 1, taken modulo 16; every row block names each of these three groups at least once. Column blocks may repeat within a row block.
All inputs are finite; a program needn't handle non-finite values.
Results may differ from a plain program's by a relative error of at most 0.015.
Values may be sent and summed in bfloat16 or wider, within the bound.
A program may use at most 192 MiB of HBM per device.

v0:
```python
import math
import jax
import jax.numpy as jnp
from jax import lax
from jax.sharding import PartitionSpec as P


def from_behind(value, axis, steps):
    count = lax.axis_size(axis)
    pairs = [(source, (source + steps) % count) for source in range(count)]
    return lax.ppermute(value, axis, pairs)


def silu_slope(value):
    sig = jax.nn.sigmoid(value)
    return sig * (1.0 + value * (1.0 - sig))


def times_transposed(left_operand, weight):
    return lax.dot_general(
        left_operand, weight, (((1,), (1,)), ((), ())), preferred_element_type=jnp.float32
    )


def local(features, tiles, columns, w_aggregate, w_self, w_middle, w_output, cotangent):
    blocks_dev, width_k, tile_size, _ = tiles.shape
    width = features.shape[1]
    groups = lax.axis_size("row")
    replicas = lax.axis_size("rep")
    panel_blocks = replicas * blocks_dev
    panel_rows = panel_blocks * tile_size
    group_id = lax.axis_index("row")
    slot_of = (columns // panel_blocks - group_id + 1) % groups
    window_index = slot_of * panel_blocks + columns % panel_blocks
    own_panel = lax.all_gather(features, "rep", axis=0, tiled=True)
    prior_panel = from_behind(own_panel, "row", 1)
    next_panel = from_behind(own_panel, "row", -1)
    window = jnp.concatenate([prior_panel, own_panel, next_panel], 0).reshape(
        3 * panel_blocks, tile_size, width
    )
    picked = window[window_index]
    summed = jnp.einsum("bkij,bkjf->bif", tiles, picked, preferred_element_type=jnp.float32)
    aggregate = summed.reshape(blocks_dev * tile_size, width).astype(jnp.bfloat16)
    pre_first = jnp.dot(aggregate, w_aggregate, preferred_element_type=jnp.float32) + jnp.dot(
        features, w_self, preferred_element_type=jnp.float32
    )
    first = jax.nn.silu(pre_first).astype(jnp.bfloat16)
    pre_second = jnp.dot(first, w_middle, preferred_element_type=jnp.float32)
    second = jax.nn.silu(pre_second).astype(jnp.bfloat16)
    updated = (
        features.astype(jnp.float32) + jnp.dot(second, w_output, preferred_element_type=jnp.float32)
    ).astype(jnp.bfloat16)
    delta_second = (times_transposed(cotangent, w_output) * silu_slope(pre_second)).astype(
        jnp.bfloat16
    )
    delta_first = (times_transposed(delta_second, w_middle) * silu_slope(pre_first)).astype(
        jnp.bfloat16
    )
    delta_aggregate = times_transposed(delta_first, w_aggregate).astype(jnp.bfloat16)
    delta_blocks = delta_aggregate.reshape(blocks_dev, tile_size, width)
    messages = jnp.einsum("bkji,bjf->bkif", tiles, delta_blocks, preferred_element_type=jnp.float32)
    spread = jnp.zeros((3 * panel_blocks, tile_size, width), jnp.float32)
    spread = spread.at[window_index.reshape(-1)].add(messages.reshape(-1, tile_size, width))
    spread = spread.reshape(3 * panel_rows, width)
    prior_part = spread[:panel_rows]
    own_part = spread[panel_rows : 2 * panel_rows]
    next_part = spread[2 * panel_rows :]
    from_next = from_behind(prior_part.astype(jnp.bfloat16), "row", -1).astype(prior_part.dtype)
    from_prior = from_behind(next_part.astype(jnp.bfloat16), "row", 1).astype(next_part.dtype)
    returned = lax.psum_scatter(
        (own_part + from_next + from_prior).astype(jnp.bfloat16),
        "rep",
        scatter_dimension=0,
        tiled=True,
    ).astype(jnp.float32)
    grad_features = (
        cotangent.astype(jnp.float32) + times_transposed(delta_first, w_self) + returned
    ).astype(jnp.bfloat16)
    total_nodes = features.shape[0] * groups * replicas
    scale = 1.0 / math.sqrt(total_nodes)
    local_output = jnp.dot(second.T, cotangent, preferred_element_type=jnp.float32)
    local_middle = jnp.dot(first.T, delta_second, preferred_element_type=jnp.float32)
    local_aggregate = jnp.dot(aggregate.T, delta_first, preferred_element_type=jnp.float32)
    local_self = jnp.dot(features.T, delta_first, preferred_element_type=jnp.float32)
    share_rows = width // replicas
    totals = lax.psum((local_output, local_middle, local_aggregate, local_self), ("row", "rep"))
    start_row = lax.axis_index("rep") * share_rows
    totals = tuple(
        (lax.dynamic_slice_in_dim(member, start_row, share_rows, 0) for member in totals)
    )
    return (
        updated,
        grad_features,
        totals[0] * scale,
        totals[1] * scale,
        totals[2] * scale,
        totals[3] * scale,
    )


def solution(mesh):
    placed = (
        P(("row", "rep"), None),
        P(("row", "rep"), None, None, None),
        P(("row", "rep"), None),
        P(),
        P(),
        P(),
        P(),
        P(("row", "rep"), None),
    )
    return jax.shard_map(
        local,
        mesh=mesh,
        in_specs=placed,
        out_specs=(
            P(("row", "rep"), None),
            P(("row", "rep"), None),
            P("rep", None),
            P("rep", None),
            P("rep", None),
            P("rep", None),
        ),
        check_vma=False,
    )
```

profile of v0, /device:TPU:4, one launch (start us, length us, event | category | flops | bytes accessed | tf_op | source)
XLA Modules:
  0.0 576.8 jit_solution(3026869364455568108)
XLA Ops:
  8.0 81.7 %all-gather.2.cloned.1.call-done = bf16[4096,512]{1,0:T(8,128)(2,1)} async-done(((bf16[256,512]{1,0:T(8,128)(2,1)}), bf16[4096,512]{1,0:T(8,128)(2,1)}) %all-gather.2.cloned.1.call-update) | async-done | bytes 4194320 | tf_op jit(solution)/shard_map/all_gather | solution.py:35
  91.0 45.0 %collective-permute-done.1 = bf16[4096,512]{1,0:T(8,128)(2,1)} collective-permute-done((bf16[4096,512]{1,0:T(8,128)(2,1)}, bf16[4096,512]{1,0:T(8,128)(2,1)}, u32[]{:S(2)}, u32[]{:S(2)}) %collective-permute-start.1) | collective-permute-done | bytes 4194336 | tf_op jit(solution)/shard_map/ppermute | solution.py:11
  136.0 1.9 collective-permute-done
  137.9 15.9 %pad_maximum_fusion = bf16[12288,512]{1,0:T(8,128)(2,1)} fusion(bf16[4096,512]{1,0:T(8,128)(2,1)} %collective-permute-done.1, bf16[4096,512]{1,0:T(8,128)(2,1)} %all-gather.2.cloned.1.call-done, bf16[4096,512]{1,0:T(8,128)(2,1)} %collective-permute-done), kind=kLoop, calls=%fused_computation.2 | loop fusion | flops 37748736 | bytes 25165824 | tf_op jit(solution)/shard_map/concatenate | solution.py:38
  153.8 5.3 gather_fusion
  159.6 1.4 fusion.15
  163.5 2.7 fusion.16
  166.2 5.4 copy.15
  171.6 11.5 %broadcast_in_dim.8 = f32[96,128,512]{2,1,0:T(8,128)} broadcast(f32[]{:T(128)} %constant.62.clone.1), dimensions={} | broadcast | bytes 25165828 | tf_op jit(solution)/shard_map/broadcast_in_dim | solution.py:62
  183.1 9.6 %scatter_fusion = f32[96,128,512]{2,1,0:T(8,128)} fusion(f32[96,128,512]{2,1,0:T(8,128)} %broadcast_in_dim.8, s32[16]{0:T(128)S(1)} %fusion.9, f32[16,128,512]{2,1,0:T(8,128)} %copy.15), kind=kCustom, calls=%fused_computation.1 | custom fusion | flops 1048576 | bytes 12582976 | tf_op jit(solution)/shard_map/scatter-add | solution.py:63
  192.7 9.3 %convert.4 = bf16[96,128,512]{2,1,0:T(8,128)(2,1)S(1)} convert(f32[96,128,512]{2,1,0:T(8,128)} %scatter_fusion) | non-fusion elementwise | flops 6291456 | bytes 37748736 | tf_op jit(solution)/shard_map/convert.1
  202.0 3.5 fusion.14
  205.5 1.7 collective-permute-start.2
  208.6 1.4 convolution_bitcast_fusion
  210.0 1.3 fusion.11
  211.3 1.4 fusion.10
  212.8 8.2 %slice.22 = f32[32,128,512]{2,1,0:T(8,128)} slice(f32[96,128,512]{2,1,0:T(8,128)} %scatter_fusion), slice={[32:64], [0:128], [0:512]} | slice | bytes 16777216 | tf_op jit(solution)/shard_map/slice | solution.py:66
  221.0 36.8 %collective-permute-done.3 = bf16[4096,512]{1,0:T(8,128)(2,1)} collective-permute-done((bf16[4096,512]{1,0:T(8,128)(2,1)}, bf16[4096,512]{1,0:T(8,128)(2,1)}, u32[]{:S(2)}, u32[]{:S(2)}) %collective-permute-start.3) | collective-permute-done | bytes 4194336 | tf_op jit(solution)/shard_map/ppermute | solution.py:11
  257.8 9.7 %fusion.1 = bf16[4096,512]{1,0:T(8,128)(2,1)} fusion(f32[32,128,512]{2,1,0:T(8,128)} %slice.22, bf16[4096,512]{1,0:T(8,128)(2,1)} %collective-permute-done.3, bf16[4096,512]{1,0:T(8,128)(2,1)} %collective-permute-done.2), kind=kLoop, calls=%fused_computation.5 | loop fusion | flops 10485760 | bytes 20971520 | tf_op jit(solution)/shard_map/convert_element_type | solution.py:71
  269.9 216.6 %all-reduce.3.cloned.1.call-done = (f32[512,512]{1,0:T(8,128)}, f32[512,512]{1,0:T(8,128)}, f32[512,512]{1,0:T(8,128)}, f32[512,512]{1,0:T(8,128)}) async-done(((f32[512,512]{1,0:T(8,128)}, f32[512,512]{1,0:T(8,128)}, f32[512,512]{1,0:T(8,128)}, f32[512,512]{1,0:T(8,128)}), (f32[512,512]{1,0:T(8,128)}, f32[512,512]{1,0:T(8,128)}, f32[512,512]{1,0:T(8,128)}, ...) | async-done | bytes 4194320 | tf_op jit(solution)/shard_map/psum | solution.py:86
  486.5 1.5 dynamic-slice_multiply_fusion.2
  488.0 1.5 dynamic-slice_multiply_fusion
  489.6 79.0 %reduce-scatter.2.cloned.1.call-done = bf16[256,512]{1,0:T(8,128)(2,1)} async-done(((bf16[4096,512]{1,0:T(8,128)(2,1)}), bf16[256,512]{1,0:T(8,128)(2,1)}) %reduce-scatter.2.cloned.1.call-update) | async-done | bytes 262160 | tf_op jit(solution)/shard_map/reduce_scatter | solution.py:70
  568.6 1.7 add_convert_fusion
  (48 shorter events, 8.8 us)
Async XLA Ops:
  7.2 152.0 %copy-start = (bf16[2,8,128,128]{3,2,1,0:T(8,128)(2,1)S(1)}, bf16[2,8,128,128]{3,2,1,0:T(8,128)(2,1)}, u32[]{:S(2)}) copy-start(bf16[2,8,128,128]{3,2,1,0:T(8,128)(2,1)} %param.9) | copy-start | bytes 1572868
  7.2 82.4 %all-gather.2.cloned.1.call-start = ((), (), s32[]{:S(2)}) async-start(), calls=%async_computation.1 | async-start | bytes 4456448 | tf_op jit(solution)/shard_map/all_gather | solution.py:35
  7.9 478.6 %all-reduce.3.cloned.1.call-start = ((), (), s32[]{:S(2)}) async-start(), calls=%async_computation.3 | async-start | bytes 8388608 | tf_op jit(solution)/shard_map/psum | solution.py:86
  89.6 46.3 %collective-permute-start.1 = (bf16[4096,512]{1,0:T(8,128)(2,1)}, bf16[4096,512]{1,0:T(8,128)(2,1)}, u32[]{:S(2)}, u32[]{:S(2)}) collective-permute-start(bf16[4096,512]{1,0:T(8,128)(2,1)} %all-gather.2.cloned.1.call-done), channel_id=1, source_target_pairs={{0,240},{16,0},{32,16},{48,32},{64,48},{80,64},{96,80},{112,96},{1... | collective-permute-start | bytes 12582920 | tf_op jit(solution)/shard_map/ppermute | solution.py:11
  89.6 48.2 %collective-permute-start = (bf16[4096,512]{1,0:T(8,128)(2,1)}, bf16[4096,512]{1,0:T(8,128)(2,1)}, u32[]{:S(2)}, u32[]{:S(2)}) collective-permute-start(bf16[4096,512]{1,0:T(8,128)(2,1)} %all-gather.2.cloned.1.call-done), channel_id=1, source_target_pairs={{0,16},{16,32},{32,48},{48,64},{64,80},{80,96},{96,112},{112,128},... | collective-permute-start | bytes 12582920 | tf_op jit(solution)/shard_map/ppermute | solution.py:11
  153.8 7.2 %copy-start.2 = (bf16[256,512]{1,0:T(8,128)(2,1)S(1)}, bf16[256,512]{1,0:T(8,128)(2,1)}, u32[]{:S(2)}) copy-start(bf16[256,512]{1,0:T(8,128)(2,1)} %param.8) | copy-start | bytes 786436
  159.1 1.9 copy-start.3
  159.1 2.2 copy-start.7
  159.1 2.5 copy-start.6
  159.2 2.5 copy-start.8
  161.7 1.5 copy-start.5
  162.1 0.7 copy-start.10
  202.0 8.0 %copy-start.11 = (bf16[256,512]{1,0:T(8,128)(2,1)S(1)}, bf16[256,512]{1,0:T(8,128)(2,1)}, u32[]{:S(2)}) copy-start(bf16[256,512]{1,0:T(8,128)(2,1)} %copy-done.10) | copy-start | bytes 786436
  205.5 52.3 %collective-permute-start.3 = (bf16[4096,512]{1,0:T(8,128)(2,1)}, bf16[4096,512]{1,0:T(8,128)(2,1)}, u32[]{:S(2)}, u32[]{:S(2)}) collective-permute-start(bf16[4096,512]{1,0:T(8,128)(2,1)} %bitcast.13), channel_id=1, source_target_pairs={{0,16},{16,32},{32,48},{48,64},{64,80},{80,96},{96,112},{112,128},... | collective-permute-start | bytes 12582920 | tf_op jit(solution)/shard_map/ppermute | solution.py:11
  205.5 52.3 %collective-permute-start.2 = (bf16[4096,512]{1,0:T(8,128)(2,1)}, bf16[4096,512]{1,0:T(8,128)(2,1)}, u32[]{:S(2)}, u32[]{:S(2)}) collective-permute-start(bf16[4096,512]{1,0:T(8,128)(2,1)} %bitcast.12), channel_id=1, source_target_pairs={{0,240},{16,0},{32,16},{48,32},{64,48},{80,64},{96,80},{112,96},{1... | collective-permute-start | bytes 12582920 | tf_op jit(solution)/shard_map/ppermute | solution.py:11
  212.7 355.9 %reduce-scatter.2.cloned.1.call-start = ((), (), s32[]{:S(2)}) async-start(), calls=%async_computation.2 | async-start | bytes 4456448 | tf_op jit(solution)/shard_map/reduce_scatter | solution.py:70
  267.5 1.0 copy-start.9
  267.5 2.1 copy-start.4
  267.5 302.8 %copy-start.1 = (bf16[2,8,128,128]{3,2,1,0:T(8,128)(2,1)S(1)}, bf16[2,8,128,128]{3,2,1,0:T(8,128)(2,1)}, u32[]{:S(2)}) copy-start(bf16[2,8,128,128]{3,2,1,0:T(8,128)(2,1)} %param.9) | copy-start | bytes 1572868
Sparse Core Ops, SparseCore 0:
  9.8 79.7 all-gather.1
  212.8 273.6 all-reduce.2
  489.2 79.3 reduce-scatter.1
where the time goes:
time: 577 us
  waiting for transfers between devices  462 us (80%)
  other arithmetic  50 us (9%)
  local copies, waits for them, and re-layouts  35.9 us (6%)
  between operations  14 us (2%)
  matrix products  13 us (2%)
    psum x1, waiting for transfers between devices, local(): lax.psum((local_output, local_middle, local_aggregate, local_self), ('row...  217 us
    ppermute x4, waiting for transfers between devices, from_behind(): return lax.ppermute(value, axis, pairs)  83.7 us
    all_gather x1, waiting for transfers between devices, local(): own_panel = lax.all_gather(features, 'rep', axis=0, tiled=True)  81.7 us
    reduce_scatter x1, waiting for transfers between devices, local(): lax.psum_scatter((own_part + from_next + from_prior).astype(jnp.bfloat16)...  79 us
    concatenate x1, other arithmetic, local(): jnp.concatenate([prior_panel, own_panel, next_panel], 0)  15.9 us
  transfers between devices with their start and end apart: 7, of which 6 were waited for; matrix products, arithmetic and copies ran while one was open for 5% of the time, Pallas kernels for 0%

commit v1 on v0

--- a/solution.py
+++ b/solution.py
@@ -32,7 +32,9 @@
     group_id = lax.axis_index("row")
     slot_of = (columns // panel_blocks - group_id + 1) % groups
     window_index = slot_of * panel_blocks + columns % panel_blocks
-    own_panel = lax.all_gather(features, "rep", axis=0, tiled=True)
+    own_panel = jnp.concatenate(
+        lax.all_to_all(jnp.stack([features] * lax.axis_size("rep")), "rep", 0, 0), axis=0
+    )
     prior_panel = from_behind(own_panel, "row", 1)
     next_panel = from_behind(own_panel, "row", -1)
     window = jnp.concatenate([prior_panel, own_panel, next_panel], 0).reshape(

time: 577 us -> 531 us (0.920)
  waiting for transfers between devices: 462 us -> 309 us
  blocking collectives: 0 us -> 104 us
    all_to_all x0 -> x1, blocking collectives: none -> 104 us  [local(): lax.all_to_all(jnp.stack([features] * lax.axis_size('rep')), 'rep', 0, 0)]
    all_gather x1 -> x0, waiting for transfers between devices: 81.7 us -> none  [local(): own_panel = lax.all_gather(features, 'rep', axis=0, tiled=True)]
    reduce_scatter x1, waiting for transfers between devices: 79 us -> 0.01 us  [local(): lax.psum_scatter((own_part + from_next + from_prior).astype(jnp.bfloat16)...]
    psum x1, waiting for transfers between devices: 217 us -> 225 us  [local(): lax.psum((local_output, local_middle, local_aggregate, local_self), ('row...]
  transfers between devices with their start and end apart: 7 -> 6, of which waited for: 6 -> 4; matrix products, arithmetic and copies ran while one was open for 5% -> 5% of each run, Pallas kernels for 0% -> 0%
where the time goes in v1:
time: 531 us; the launch traced here: 530 us
  waiting for transfers between devices  309 us (58%)
  blocking collectives  104 us (20%)
  other arithmetic  49.4 us (9%)
  local copies, waits for them, and re-layouts  37.3 us (7%)
  between operations  15.7 us (3%)
  matrix products  13 us (2%)
    psum x1, waiting for transfers between devices, local(): lax.psum((local_output, local_middle, local_aggregate, local_self), ('row...  225 us
    all_to_all x1, blocking collectives, local(): lax.all_to_all(jnp.stack([features] * lax.axis_size('rep')), 'rep', 0, 0)  104 us
    ppermute x4, waiting for transfers between devices, from_behind(): return lax.ppermute(value, axis, pairs)  83.9 us
    concatenate x1, other arithmetic, local(): jnp.concatenate([prior_panel, own_panel, next_panel], 0)  15.9 us
    broadcast_in_dim x1, local copies, waits for them, and re-layouts, local(): spread = jnp.zeros((3 * panel_blocks, tile_size, width), jnp.float32)  11.5 us
  transfers between devices with their start and end apart: 6, of which 4 were waited for; matrix products, arithmetic and copies ran while one was open for 5% of the time, Pallas kernels for 0%

profile of v1, /device:TPU:4, one launch (start us, length us, event | category | flops | bytes accessed | tf_op | source)
XLA Modules:
  0.0 530.1 jit_solution(7137919601561487912)
XLA Ops:
  8.1 1.4 stack.2
  9.5 103.8 %all_to_all.5 = bf16[16,256,512]{2,1,0:T(8,128)(2,1)} all-to-all(bf16[16,256,512]{2,1,0:T(8,128)(2,1)S(1)} %stack.2), channel_id=1, replica_groups=mesh['row'=16,'rep'=16] {'rep'}, dimensions={0} | all-to-all | bytes 8388608 | tf_op jit(solution)/shard_map/all_to_all | solution.py:36
  114.0 45.6 %collective-permute-done.1 = bf16[4096,512]{1,0:T(8,128)(2,1)} collective-permute-done((bf16[4096,512]{1,0:T(8,128)(2,1)}, bf16[4096,512]{1,0:T(8,128)(2,1)}, u32[]{:S(2)}, u32[]{:S(2)}) %collective-permute-start.1) | collective-permute-done | bytes 4194336 | tf_op jit(solution)/shard_map/ppermute | solution.py:11
  159.7 1.9 collective-permute-done
  161.6 15.9 %pad_maximum_fusion = bf16[12288,512]{1,0:T(8,128)(2,1)} fusion(bf16[4096,512]{1,0:T(8,128)(2,1)} %collective-permute-done.1, bf16[4096,512]{1,0:T(8,128)(2,1)} %bitcast, bf16[4096,512]{1,0:T(8,128)(2,1)} %collective-permute-done), kind=kLoop, calls=%fused_computation.2 | loop fusion | flops 37748736 | bytes 25165824 | tf_op jit(solution)/shard_map/concatenate | solution.py:40
  177.5 5.3 gather_fusion
  183.3 1.4 fusion.15
  187.2 2.7 fusion.16
  189.9 5.4 %copy.15 = f32[16,128,512]{2,1,0:T(8,128)} copy(f32[16,128,512]{1,2,0:T(8,128)} %bitcast.56) | data formatting | bytes 8388608 | tf_op jit(solution)/shard_map/reshape | solution.py:65
  195.3 11.5 %broadcast_in_dim.8 = f32[96,128,512]{2,1,0:T(8,128)} broadcast(f32[]{:T(128)} %constant.62.clone.1), dimensions={} | broadcast | bytes 25165828 | tf_op jit(solution)/shard_map/broadcast_in_dim | solution.py:64
  206.8 9.6 %scatter_fusion = f32[96,128,512]{2,1,0:T(8,128)} fusion(f32[96,128,512]{2,1,0:T(8,128)} %broadcast_in_dim.8, s32[16]{0:T(128)S(1)} %fusion.9, f32[16,128,512]{2,1,0:T(8,128)} %copy.15), kind=kCustom, calls=%fused_computation.1 | custom fusion | flops 1048576 | bytes 12582976 | tf_op jit(solution)/shard_map/scatter-add | solution.py:65
  216.5 9.3 %convert.4 = bf16[96,128,512]{2,1,0:T(8,128)(2,1)S(1)} convert(f32[96,128,512]{2,1,0:T(8,128)} %scatter_fusion) | non-fusion elementwise | flops 6291456 | bytes 37748736 | tf_op jit(solution)/shard_map/convert.1
  225.8 3.5 fusion.14
  229.3 1.7 collective-permute-start.2
  232.4 1.4 convolution_bitcast_fusion
  233.7 1.3 fusion.11
  235.1 1.4 fusion.10
  236.5 8.2 %slice.22 = f32[32,128,512]{2,1,0:T(8,128)} slice(f32[96,128,512]{2,1,0:T(8,128)} %scatter_fusion), slice={[32:64], [0:128], [0:512]} | slice | bytes 16777216 | tf_op jit(solution)/shard_map/slice | solution.py:68
  244.7 36.4 %collective-permute-done.3 = bf16[4096,512]{1,0:T(8,128)(2,1)} collective-permute-done((bf16[4096,512]{1,0:T(8,128)(2,1)}, bf16[4096,512]{1,0:T(8,128)(2,1)}, u32[]{:S(2)}, u32[]{:S(2)}) %collective-permute-start.3) | collective-permute-done | bytes 4194336 | tf_op jit(solution)/shard_map/ppermute | solution.py:11
  281.1 9.7 %fusion.1 = bf16[4096,512]{1,0:T(8,128)(2,1)} fusion(f32[32,128,512]{2,1,0:T(8,128)} %slice.22, bf16[4096,512]{1,0:T(8,128)(2,1)} %collective-permute-done.3, bf16[4096,512]{1,0:T(8,128)(2,1)} %collective-permute-done.2), kind=kLoop, calls=%fused_computation.5 | loop fusion | flops 10485760 | bytes 20971520 | tf_op jit(solution)/shard_map/convert_element_type | solution.py:73
  293.3 224.6 %all-reduce.3.cloned.1.call-done = (f32[512,512]{1,0:T(8,128)}, f32[512,512]{1,0:T(8,128)}, f32[512,512]{1,0:T(8,128)}, f32[512,512]{1,0:T(8,128)}) async-done(((f32[512,512]{1,0:T(8,128)}, f32[512,512]{1,0:T(8,128)}, f32[512,512]{1,0:T(8,128)}, f32[512,512]{1,0:T(8,128)}), (f32[512,512]{1,0:T(8,128)}, f32[512,512]{1,0:T(8,128)}, f32[512,512]{1,0:T(8,128)}, ...) | async-done | bytes 4194320 | tf_op jit(solution)/shard_map/psum | solution.py:88
  517.9 1.5 dynamic-slice_multiply_fusion.2
  519.4 1.5 dynamic-slice_multiply_fusion
  520.9 1.7 add_convert_fusion
  (49 shorter events, 7.5 us)
Async XLA Ops:
  8.0 174.8 %copy-start = (bf16[2,8,128,128]{3,2,1,0:T(8,128)(2,1)S(1)}, bf16[2,8,128,128]{3,2,1,0:T(8,128)(2,1)}, u32[]{:S(2)}) copy-start(bf16[2,8,128,128]{3,2,1,0:T(8,128)(2,1)} %param.9) | copy-start | bytes 1572868
  8.0 509.9 %all-reduce.3.cloned.1.call-start = ((), (), s32[]{:S(2)}) async-start(), calls=%async_computation.3 | async-start | bytes 8388608 | tf_op jit(solution)/shard_map/psum | solution.py:88
  9.5 104.4 %copy-start.7 = (s32[2,8]{1,0:T(2,128)S(1)}, s32[2,8]{1,0:T(2,128)}, u32[]{:S(2)}) copy-start(s32[2,8]{1,0:T(2,128)} %param.10) | copy-start | bytes 196
  113.3 46.3 %collective-permute-start.1 = (bf16[4096,512]{1,0:T(8,128)(2,1)}, bf16[4096,512]{1,0:T(8,128)(2,1)}, u32[]{:S(2)}, u32[]{:S(2)}) collective-permute-start(bf16[4096,512]{1,0:T(8,128)(2,1)} %bitcast), channel_id=1, source_target_pairs={{0,240},{16,0},{32,16},{48,32},{64,48},{80,64},{96,80},{112,96},{1... | collective-permute-start | bytes 12582920 | tf_op jit(solution)/shard_map/ppermute | solution.py:11
  113.3 48.2 %collective-permute-start = (bf16[4096,512]{1,0:T(8,128)(2,1)}, bf16[4096,512]{1,0:T(8,128)(2,1)}, u32[]{:S(2)}, u32[]{:S(2)}) collective-permute-start(bf16[4096,512]{1,0:T(8,128)(2,1)} %bitcast), channel_id=1, source_target_pairs={{0,16},{16,32},{32,48},{48,64},{64,80},{80,96},{96,112},{112,128},... | collective-permute-start | bytes 12582920 | tf_op jit(solution)/shard_map/ppermute | solution.py:11
  177.5 7.2 %copy-start.2 = (bf16[256,512]{1,0:T(8,128)(2,1)S(1)}, bf16[256,512]{1,0:T(8,128)(2,1)}, u32[]{:S(2)}) copy-start(bf16[256,512]{1,0:T(8,128)(2,1)} %param.8) | copy-start | bytes 786436
  182.8 1.9 copy-start.3
  182.8 2.2 copy-start.8
  182.8 2.5 copy-start.6
  182.9 2.5 copy-start.9
  185.4 1.5 copy-start.5
  185.8 0.7 copy-start.11
  225.7 8.0 %copy-start.12 = (bf16[256,512]{1,0:T(8,128)(2,1)S(1)}, bf16[256,512]{1,0:T(8,128)(2,1)}, u32[]{:S(2)}) copy-start(bf16[256,512]{1,0:T(8,128)(2,1)} %copy-done.11) | copy-start | bytes 786436
  229.3 51.8 %collective-permute-start.3 = (bf16[4096,512]{1,0:T(8,128)(2,1)}, bf16[4096,512]{1,0:T(8,128)(2,1)}, u32[]{:S(2)}, u32[]{:S(2)}) collective-permute-start(bf16[4096,512]{1,0:T(8,128)(2,1)} %bitcast.14), channel_id=1, source_target_pairs={{0,16},{16,32},{32,48},{48,64},{64,80},{80,96},{96,112},{112,128},... | collective-permute-start | bytes 12582920 | tf_op jit(solution)/shard_map/ppermute | solution.py:11
  229.3 51.8 %collective-permute-start.2 = (bf16[4096,512]{1,0:T(8,128)(2,1)}, bf16[4096,512]{1,0:T(8,128)(2,1)}, u32[]{:S(2)}, u32[]{:S(2)}) collective-permute-start(bf16[4096,512]{1,0:T(8,128)(2,1)} %bitcast.13), channel_id=1, source_target_pairs={{0,240},{16,0},{32,16},{48,32},{64,48},{80,64},{96,80},{112,96},{1... | collective-permute-start | bytes 12582920 | tf_op jit(solution)/shard_map/ppermute | solution.py:11
  236.5 284.5 %reduce-scatter.2.cloned.1.call-start = ((), (), s32[]{:S(2)}) async-start(), calls=%async_computation.2 | async-start | bytes 4456448 | tf_op jit(solution)/shard_map/reduce_scatter | solution.py:72
  290.9 1.1 copy-start.10
  290.9 2.1 copy-start.4
  290.9 231.8 %copy-start.1 = (bf16[2,8,128,128]{3,2,1,0:T(8,128)(2,1)S(1)}, bf16[2,8,128,128]{3,2,1,0:T(8,128)(2,1)}, u32[]{:S(2)}) copy-start(bf16[2,8,128,128]{3,2,1,0:T(8,128)(2,1)} %param.9) | copy-start | bytes 1572868
Sparse Core Ops, SparseCore 0:
  236.6 281.2 all-reduce.2
Sparse Core Ops, SparseCore 1:
  291.0 90.1 reduce-scatter.1
